TPU v7x, 32 devices: a whole 2x2x4 slice. The times are simulated.
32 devices in a mesh: leaf: 16 (over z, y, x), cone: 2 (over core).
Axes of the slice: x: 2, y: 2, z: 4, core: 2. Of those that a mesh axis runs over, the one named last changes fastest.
Arguments:
- coefficients: bfloat16 [128, 4, 3, 32, 256], P('leaf', 'cone'), may hold values from -6 to 6
- local_to_target: bfloat16 [128, 4, 256, 768], P('leaf', 'cone'), may hold values from -0.1875 to 0.1875
- send_map: int32 [16, 16, 32], P('leaf'), may hold values from -1 to 255, as said below
- test_weight: bfloat16 [16, 16, 32, 108], P('leaf'), may hold values from -1 to 1
- slot_edge: int32 [3, 16, 16, 32], P(None, 'leaf'), may hold values from -1 to 383, as said below
- shared_edges: int32 [16, 2, 32], P('leaf'), may hold values from 0 to 383, as said below
Outputs:
- tested: float32 [2, 32, 6144], P(None, 'cone', 'leaf')
Inputs may be any that keep to these rules, and one draw needn't show every extreme that they name: Each of the 256 triangles of a leaf device s stands in exactly one slot of send_map[s]; every other slot is -1. In every draw, each leaf device fills all 32 slots of its block to some owner. slot_edge[e, d, s, n] is -1 exactly where send_map[s, d, n] is -1. The 64 numbers of shared_edges[d] are distinct.
All inputs are finite; a program needn't handle non-finite values.
Results may differ from a plain program's by a relative error of at most 0.0029.
Values may be sent and summed in bfloat16 or wider, within the bound.
A program may use at most 64 MiB of HBM per device.

v0:
```python
import jax
import jax.numpy as jnp
from jax import lax
from jax.sharding import PartitionSpec as P

QUAD = 12
TRI_LEAF = 32
EDGE_DEV = 384


def extended(array, sides, width):
    for axis, dim in sides:
        peers, length = (lax.axis_size(axis), array.shape[dim])
        up = [(i, (i + 1) % peers) for i in range(peers - 1)]
        down = [(j, i) for i, j in up]
        last = lax.slice_in_dim(array, length - width, length, axis=dim)
        leading = lax.slice_in_dim(array, 0, width, axis=dim)
        before = lax.ppermute(last, axis, up)
        after = lax.ppermute(leading, axis, down)
        array = jnp.concatenate([before, array, after], axis=dim)
    return array


def tested_slots(weights, fields, rhs_count, result_form):
    peer_count, capacity = (weights.shape[0], weights.shape[1])
    weight_view = weights.reshape(peer_count, capacity, 3, QUAD, 3)
    field_view = fields.reshape(peer_count, capacity, QUAD, 2, 3, rhs_count)
    return jnp.einsum(
        "scepk,scpikh->" + result_form, weight_view, field_view, preferred_element_type=jnp.float32
    )


def body(coefficients, local_to_target, send_map, test_weight, slot_edge, shared_edges):
    partial_field = jnp.einsum(
        "lkchr,lkrq->lqch", coefficients, local_to_target, preferred_element_type=jnp.float32
    )
    cone_count = lax.axis_size("cone")
    rhs_count = partial_field.shape[3] // cone_count
    summed = lax.psum(partial_field, "cone")
    rhs_share = lax.dynamic_slice_in_dim(summed, lax.axis_index("cone") * rhs_count, rhs_count, 3)
    rhs_share = rhs_share.astype(jnp.bfloat16)
    leaf_count = rhs_share.shape[0]
    tri_rows = rhs_share.reshape(leaf_count * TRI_LEAF, -1)
    send_rows = send_map[0]
    is_live = send_rows >= 0
    safe_rows = jnp.where(is_live, send_rows, 0)
    picked = tri_rows[safe_rows]
    outgoing = jnp.where(is_live[:, :, None], picked, jnp.zeros((), jnp.bfloat16))
    weights = test_weight[0]
    arrived = lax.all_to_all(outgoing, "leaf", split_axis=0, concat_axis=0, tiled=True)
    partial_value = tested_slots(weights, arrived, rhs_count, "escih")
    edge_ids = slot_edge[:, 0].reshape(-1)
    values = partial_value.reshape(-1, 2 * rhs_count)
    onehot = (edge_ids[:, None] == jnp.arange(EDGE_DEV, dtype=jnp.int32)[None, :]).astype(
        jnp.float32
    )
    edge_sum = jnp.einsum(
        "ra,re->ae",
        values,
        onehot,
        precision=lax.Precision.HIGHEST,
        preferred_element_type=jnp.float32,
    )
    lower_ids = shared_edges[0, 0]
    upper_ids = shared_edges[0, 1]
    share_width = lower_ids.shape[0]
    rim_values = jnp.concatenate([edge_sum[:, lower_ids], edge_sum[:, upper_ids]], axis=1)
    padded = extended(rim_values, (("leaf", 1),), share_width)
    total = (
        edge_sum.at[:, lower_ids]
        .add(padded[:, :share_width])
        .at[:, upper_ids]
        .add(padded[:, 3 * share_width :])
    )
    return total.reshape(2, rhs_count, -1)


def solution(mesh):
    placed = (
        P("leaf", "cone", None, None, None),
        P("leaf", "cone", None, None),
        P("leaf", None, None),
        P("leaf", None, None, None),
        P(None, "leaf", None, None),
        P("leaf", None, None),
    )
    return jax.shard_map(
        body, mesh=mesh, in_specs=placed, out_specs=P(None, "cone", "leaf"), check_vma=False
    )
```

profile of v0, /device:TPU:6, one launch (start us, length us, event | category | flops | bytes accessed | tf_op | source)
XLA Modules:
  0.0 120.5 jit_solution(16568541062340450514)
XLA Ops:
  0.0 0.8 compare_select_fusion
  0.8 0.7 compare_bitcast_fusion
  1.5 5.3 %fusion.3 = f32[8,768,3,32]{1,3,2,0:T(8,128)} fusion(bf16[8,2,3,32,256]{4,3,2,1,0:T(8,128)(2,1)S(1)} %copy-done, bf16[8,2,256,768]{3,2,1,0:T(8,128)(2,1)} %param.7), kind=kOutput, calls=%fused_computation.9 | convolution fusion | flops 603979776 | bytes 9437184 | tf_op jit(solution)/shard_map/lkchr,lkrq->lqch/dot_general | solution.py:34
  6.8 10.3 %all-reduce.1 = bf16[8,768,3,32]{1,3,2,0:T(8,128)(2,1)S(1)} all-reduce(f32[8,768,3,32]{1,3,2,0:T(8,128)} %fusion.3), channel_id=1, replica_groups=mesh['leaf'=16,'cone'=2] {'cone'}, use_global_device_ids=true, to_apply=%region_0.0 | all-reduce | flops 589824 | bytes 3538944 | tf_op jit(solution)/shard_map/psum | solution.py:39
  17.1 6.7 %copy.25 = bf16[8,768,3,16]{3,2,1,0:T(4,128)(2,1)} copy(bf16[8,768,3,16]{1,3,2,0:T(8,128)(2,1)S(1)} %dynamic-slice_convert_fusion) | data formatting | bytes 1179648 | tf_op jit(solution)/shard_map/convert_element_type | solution.py:41
  23.9 9.3 %reshape.102 = bf16[256,1152]{1,0:T(8,128)(2,1)S(1)} reshape(bf16[8,768,3,16]{3,2,1,0:T(4,128)(2,1)} %copy.25) | data formatting | bytes 1179648 | tf_op jit(solution)/shard_map/reshape | solution.py:43
  33.3 2.1 %gather_fusion = bf16[512,1152]{1,0:T(8,128)(2,1)S(1)} fusion(bf16[256,1152]{1,0:T(8,128)(2,1)S(1)} %reshape.102, s32[1024]{0:T(1024)S(1)} %pad_clamp_fusion.2), kind=kCustom, calls=%fused_computation | custom fusion | bytes 2361344 | tf_op jit(solution)/shard_map/gather | solution.py:47
  35.4 1.2 %broadcast_select_fusion = bf16[16,32,1152]{2,1,0:T(8,128)(2,1)} fusion(bf16[16,32,1152]{2,1,0:T(8,128)(2,1)S(1)} %bitcast.58, pred[16,32]{1,0:T(8,128)(4,1)S(1)} %compare_bitcast_fusion), kind=kLoop, calls=%fused_computation.13 | loop fusion | flops 589824 | bytes 2359808 | tf_op jit(solution)/shard_map/jit(_where)/select_n | solution.py:48
  36.6 7.4 %all-to-all-start = ((bf16[16,32,1152]{2,1,0:T(8,128)(2,1)}), bf16[16,32,1152]{2,1,0:T(8,128)(2,1)S(1)}, u32[]{:S(2)}, u32[]{:S(2)}) async-start(bf16[16,32,1152]{2,1,0:T(8,128)(2,1)} %broadcast_select_fusion), calls=%async_computation | async-start | bytes 2359296 | tf_op jit(solution)/shard_map/all_to_all | solution.py:50
  44.4 2.5 %copy.37 = bf16[16,32,3,12,3,1]{3,2,4,5,1,0:T(4,128)(2,1)} copy(bf16[16,32,3,12,3,1]{1,0,4,3,2,5:T(8,128)(2,1)S(1)} %bitcast.59) | data formatting | bytes 221184 | tf_op jit(solution)/shard_map/reshape;squeeze | solution.py:26
  47.1 23.8 %all-to-all-done = bf16[16,32,1152]{2,1,0:T(8,128)(2,1)S(1)} async-done(((bf16[16,32,1152]{2,1,0:T(8,128)(2,1)}), bf16[16,32,1152]{2,1,0:T(8,128)(2,1)S(1)}, u32[]{:S(2)}, u32[]{:S(2)}) %all-to-all-start) | async-done | bytes 1179680 | tf_op jit(solution)/shard_map/all_to_all | solution.py:50
  70.9 3.3 %copy.26 = bf16[16,32,1152]{1,2,0:T(8,128)(2,1)} copy(bf16[16,32,1152]{2,1,0:T(8,128)(2,1)S(1)} %all-to-all-done) | data formatting | bytes 2359296 | tf_op jit(solution)/shard_map/all_to_all | solution.py:50
  74.2 19.7 %copy.28 = bf16[16,32,12,2,3,16]{5,2,4,3,1,0:T(8,128)(2,1)} copy(bf16[16,32,12,2,3,16]{1,5,4,3,2,0:T(8,128)(2,1)} %bitcast.57) | data formatting | bytes 2359296 | tf_op jit(solution)/shard_map/reshape | solution.py:27
  93.9 6.6 %convolution_bitcast_fusion = f32[3,16,32,2,16]{4,0,3,2,1:T(4,128)} fusion(bf16[16,32,12,2,3,16]{5,2,4,3,1,0:T(8,128)(2,1)} %copy.28, bf16[16,32,3,12,3,1]{3,2,4,5,1,0:T(4,128)(2,1)S(1)} %copy-done.1), kind=kOutput, calls=%fused_computation.10 | convolution fusion | flops 3538944 | bytes 1486848 | tf_op jit(solution)/shard_map/scepk,scpikh->escih/dot_general | solution.py:28
  100.5 1.8 %copy.30 = f32[3,16,32,2,16]{2,1,0,4,3:T(8,128)S(1)} copy(f32[3,16,32,2,16]{4,0,3,2,1:T(4,128)} %convolution_bitcast_fusion) | data formatting | bytes 393216 | tf_op jit(solution)/shard_map/scepk,scpikh->escih/transpose | solution.py:28
  102.7 2.2 %fusion.2 = f32[32,384]{0,1:T(8,128)S(1)} fusion(f32[1536,32]{0,1:T(8,128)S(1)} %reshape.104, s32[1536]{0:T(1024)S(1)} %eq.15), kind=kOutput, calls=%fused_computation.8 | convolution fusion | flops 227082240 | bytes 251904 | tf_op jit(solution)/shard_map/ra,re->ae/dot_general | solution.py:57
  104.9 0.6 gather_fusion.1
  105.5 5.4 %collective-permute-start = (f32[32,32]{0,1:T(8,128)S(1)}, f32[32,32]{0,1:T(8,128)S(1)}, u32[]{:S(2)}, u32[]{:S(2)}) collective-permute-start(f32[32,32]{0,1:T(8,128)S(1)} %bitcast.61), channel_id=1, source_target_pairs={{0,2},{2,4},{4,6},{6,8},{8,10},{10,12},{12,14},{14,16},{16,18},{18... | collective-permute-start | bytes 12296 | tf_op jit(solution)/shard_map/ppermute | solution.py:18
  111.0 0.6 gather_fusion.2
  111.5 1.9 %collective-permute-start.1 = (f32[32,32]{0,1:T(8,128)S(1)}, f32[32,32]{0,1:T(8,128)S(1)}, u32[]{:S(2)}, u32[]{:S(2)}) collective-permute-start(f32[32,32]{0,1:T(8,128)S(1)} %bitcast.60), channel_id=1, source_target_pairs={{2,0},{4,2},{6,4},{8,6},{10,8},{12,10},{14,12},{16,14},{18,16},{20... | collective-permute-start | bytes 12296 | tf_op jit(solution)/shard_map/ppermute | solution.py:19
  113.5 0.8 scatter_custom_fusion
  114.3 4.6 %collective-permute-done.1 = f32[32,32]{0,1:T(8,128)S(1)} collective-permute-done((f32[32,32]{0,1:T(8,128)S(1)}, f32[32,32]{0,1:T(8,128)S(1)}, u32[]{:S(2)}, u32[]{:S(2)}) %collective-permute-start.1) | collective-permute-done | bytes 4128 | tf_op jit(solution)/shard_map/ppermute | solution.py:19
  119.0 0.8 scatter_custom_fusion.1
  119.8 0.7 copy.34
  (19 shorter events, 1.0 us)
Async XLA Ops:
  0.0 1.5 %copy-start = (bf16[8,2,3,32,256]{4,3,2,1,0:T(8,128)(2,1)S(1)}, bf16[8,2,3,32,256]{4,3,2,1,0:T(8,128)(2,1)}, u32[]{:S(2)}) copy-start(bf16[8,2,3,32,256]{4,3,2,1,0:T(8,128)(2,1)} %param.6) | copy-start | bytes 2359300
  35.4 8.6 %copy-start.2 = (bf16[1,16,32,108]{3,2,1,0:T(8,128)(2,1)S(1)}, bf16[1,16,32,108]{3,2,1,0:T(8,128)(2,1)}, u32[]{:S(2)}) copy-start(bf16[1,16,32,108]{3,2,1,0:T(8,128)(2,1)} %param.9) | copy-start | bytes 331780
  36.6 10.3 %copy-start.3 = (s32[3,1,16,32]{3,2,1,0:T(8,128)S(1)}, s32[3,1,16,32]{3,2,1,0:T(8,128)}, u32[]{:S(2)}) copy-start(s32[3,1,16,32]{3,2,1,0:T(8,128)} %param.10) | copy-start | bytes 18436
  36.6 10.4 %copy-start.4 = (s32[1,2,32]{2,1,0:T(2,128)S(1)}, s32[1,2,32]{2,1,0:T(2,128)}, u32[]{:S(2)}) copy-start(s32[1,2,32]{2,1,0:T(2,128)} %param.11) | copy-start | bytes 772
  36.6 34.2 %all-to-all-start = ((bf16[16,32,1152]{2,1,0:T(8,128)(2,1)}), bf16[16,32,1152]{2,1,0:T(8,128)(2,1)S(1)}, u32[]{:S(2)}, u32[]{:S(2)}) async-start(bf16[16,32,1152]{2,1,0:T(8,128)(2,1)} %broadcast_select_fusion), calls=%async_computation | async-start | bytes 2359296 | tf_op jit(solution)/shard_map/all_to_all | solution.py:50
  74.2 19.7 %copy-start.1 = (bf16[16,32,3,12,3,1]{3,2,4,5,1,0:T(4,128)(2,1)S(1)}, bf16[16,32,3,12,3,1]{3,2,4,5,1,0:T(4,128)(2,1)}, u32[]{:S(2)}) copy-start(bf16[16,32,3,12,3,1]{3,2,4,5,1,0:T(4,128)(2,1)} %copy.37) | copy-start | bytes 331780
  105.5 7.9 %collective-permute-start = (f32[32,32]{0,1:T(8,128)S(1)}, f32[32,32]{0,1:T(8,128)S(1)}, u32[]{:S(2)}, u32[]{:S(2)}) collective-permute-start(f32[32,32]{0,1:T(8,128)S(1)} %bitcast.61), channel_id=1, source_target_pairs={{0,2},{2,4},{4,6},{6,8},{8,10},{10,12},{12,14},{14,16},{16,18},{18... | collective-permute-start | bytes 12296 | tf_op jit(solution)/shard_map/ppermute | solution.py:18
  111.5 7.4 %collective-permute-start.1 = (f32[32,32]{0,1:T(8,128)S(1)}, f32[32,32]{0,1:T(8,128)S(1)}, u32[]{:S(2)}, u32[]{:S(2)}) collective-permute-start(f32[32,32]{0,1:T(8,128)S(1)} %bitcast.60), channel_id=1, source_target_pairs={{2,0},{4,2},{6,4},{8,6},{10,8},{12,10},{14,12},{16,14},{18,16},{20... | collective-permute-start | bytes 12296 | tf_op jit(solution)/shard_map/ppermute | solution.py:19
where the time goes:
time: 121 us
  local copies, waits for them, and re-layouts  48.4 us (40%)
  waiting for transfers between devices  28.4 us (23%)
  starting transfers between devices  14.7 us (12%)
  matrix products  14.2 us (12%)
  blocking collectives  10.3 us (9%)
  other arithmetic  4.39 us (4%)
    all_to_all x1, waiting for transfers between devices, body(): lax.all_to_all(outgoing, 'leaf', split_axis=0, concat_axis=0, tiled=True)  23.8 us
    reshape x1, local copies, waits for them, and re-layouts, tested_slots(): field_view = fields.reshape(peer_count, capacity, QUAD, 2, 3, rhs_count)  19.7 us
    psum x1, blocking collectives, body(): summed = lax.psum(partial_field, 'cone')  10.3 us
    reshape x1, local copies, waits for them, and re-layouts, body(): tri_rows = rhs_share.reshape(leaf_count * TRI_LEAF, -1)  9.31 us
    all_to_all x1, starting transfers between devices, body(): lax.all_to_all(outgoing, 'leaf', split_axis=0, concat_axis=0, tiled=True)  7.4 us
    convert_element_type x2, local copies, waits for them, and re-layouts, body(): rhs_share = rhs_share.astype(jnp.bfloat16)  6.78 us
    dot_general x1, matrix products, tested_slots(): jnp.einsum('scepk,scpikh->' + result_form, weight_view, field_view, prefe...  6.63 us
    ppermute x1, starting transfers between devices, extended(): before = lax.ppermute(last, axis, up)  5.42 us
  transfers between devices with their start and end apart: 3, of which 2 were waited for; matrix products, arithmetic and copies ran while one was open for 4% of the time, Pallas kernels for 0%

commit v1 on v0

--- a/solution.py
+++ b/solution.py
@@ -36,7 +36,8 @@
     )
     cone_count = lax.axis_size("cone")
     rhs_count = partial_field.shape[3] // cone_count
-    summed = lax.psum(partial_field, "cone")
+    parts = lax.all_gather(partial_field, "cone", axis=0, tiled=False)
+    summed = parts.sum(axis=0)
     rhs_share = lax.dynamic_slice_in_dim(summed, lax.axis_index("cone") * rhs_count, rhs_count, 3)
     rhs_share = rhs_share.astype(jnp.bfloat16)
     leaf_count = rhs_share.shape[0]

time: 121 us -> 142 us (1.17)
  waiting for transfers between devices: 28.4 us -> 43.7 us
  between operations: 0.12 us -> 13.5 us
  blocking collectives: 10.3 us -> 0 us
  local copies, waits for them, and re-layouts: 48.4 us -> 50.1 us
    all_gather x0 -> x1, waiting for transfers between devices: none -> 15.3 us  [body(): parts = lax.all_gather(partial_field, 'cone', axis=0, tiled=False)]
    psum x1 -> x0, blocking collectives: 10.3 us -> none  [body(): summed = lax.psum(partial_field, 'cone')]
    reduce_sum x0 -> x1, other arithmetic: none -> 2.85 us  [body(): summed = parts.sum(axis=0)]
    unnamed x11 -> x13, local copies, waits for them, and re-layouts: 0.41 us -> 2.21 us
  transfers between devices with their start and end apart: 3 -> 4, of which waited for: 2 -> 3; matrix products, arithmetic and copies ran while one was open for 4% -> 3% of each run, Pallas kernels for 0% -> 0%
where the time goes in v1:
time: 142 us
  local copies, waits for them, and re-layouts  50.1 us (35%)
  waiting for transfers between devices  43.7 us (31%)
  starting transfers between devices  14.4 us (10%)
  matrix products  14.2 us (10%)
  between operations  13.5 us (10%)
  other arithmetic  5.78 us (4%)
    all_to_all x1, waiting for transfers between devices, body(): lax.all_to_all(outgoing, 'leaf', split_axis=0, concat_axis=0, tiled=True)  23.7 us
    reshape x1, local copies, waits for them, and re-layouts, tested_slots(): field_view = fields.reshape(peer_count, capacity, QUAD, 2, 3, rhs_count)  19.6 us
    all_gather x1, waiting for transfers between devices, body(): parts = lax.all_gather(partial_field, 'cone', axis=0, tiled=False)  15.3 us
    reshape x1, local copies, waits for them, and re-layouts, body(): tri_rows = rhs_share.reshape(leaf_count * TRI_LEAF, -1)  9.31 us
    all_to_all x1, starting transfers between devices, body(): lax.all_to_all(outgoing, 'leaf', split_axis=0, concat_axis=0, tiled=True)  7.11 us
    convert_element_type x2, local copies, waits for them, and re-layouts, body(): rhs_share = rhs_share.astype(jnp.bfloat16)  6.76 us
    dot_general x1, matrix products, tested_slots(): jnp.einsum('scepk,scpikh->' + result_form, weight_view, field_view, prefe...  6.63 us
    ppermute x1, starting transfers between devices, extended(): before = lax.ppermute(last, axis, up)  5.4 us
  transfers between devices with their start and end apart: 4, of which 3 were waited for; matrix products, arithmetic and copies ran while one was open for 3% of the time, Pallas kernels for 0%

profile of v1, /device:TPU:6, one launch (start us, length us, event | category | flops | bytes accessed | tf_op | source)
XLA Modules:
  0.0 141.7 jit_solution(10444902585395165806)
XLA Ops:
  6.5 1.1 copy-done
  7.7 5.3 %fusion.3 = f32[8,768,3,32]{1,3,2,0:T(8,128)} fusion(bf16[8,2,3,32,256]{4,3,2,1,0:T(8,128)(2,1)S(1)} %copy-done, bf16[8,2,256,768]{3,2,1,0:T(8,128)(2,1)} %param.7), kind=kOutput, calls=%fused_computation.9 | convolution fusion | flops 603979776 | bytes 9437184 | tf_op jit(solution)/shard_map/lkchr,lkrq->lqch/dot_general | solution.py:34
  13.0 0.7 copy-done.3
  13.8 15.3 %all-gather.3.cloned.1.call-done = f32[16,768,3,32]{1,3,2,0:T(8,128)} async-done(((f32[8,768,3,32]{1,3,2,0:T(8,128)}), f32[16,768,3,32]{1,3,2,0:T(8,128)}) %all-gather.3.cloned.1.call-update) | async-done | bytes 4718608 | tf_op jit(solution)/shard_map/all_gather | solution.py:39
  29.1 2.8 %reduce_sum.9 = bf16[8,768,3,32]{1,3,2,0:T(8,128)(2,1)S(1)} reduce(f32[2,8,768,3,32]{2,4,3,1,0:T(8,128)} %bitcast.60, f32[]{:T(128)} %constant.9.clone.1), dimensions={0}, to_apply=%region_0.0 | reduce | flops 589824 | bytes 5898244 | tf_op jit(solution)/shard_map/reduce_sum | solution.py:40
  32.0 6.7 %copy.24 = bf16[8,768,3,16]{3,2,1,0:T(4,128)(2,1)} copy(bf16[8,768,3,16]{1,3,2,0:T(8,128)(2,1)S(1)} %dynamic-slice_convert_fusion) | data formatting | bytes 1179648 | tf_op jit(solution)/shard_map/convert_element_type | solution.py:42
  38.7 9.3 %reshape.102 = bf16[256,1152]{1,0:T(8,128)(2,1)S(1)} reshape(bf16[8,768,3,16]{3,2,1,0:T(4,128)(2,1)} %copy.24) | data formatting | bytes 1179648 | tf_op jit(solution)/shard_map/reshape | solution.py:44
  48.0 2.1 %gather_fusion = bf16[512,1152]{1,0:T(8,128)(2,1)S(1)} fusion(bf16[256,1152]{1,0:T(8,128)(2,1)S(1)} %reshape.102, s32[1024]{0:T(1024)S(1)} %pad_clamp_fusion.2), kind=kCustom, calls=%fused_computation | custom fusion | bytes 2361344 | tf_op jit(solution)/shard_map/gather | solution.py:48
  50.2 1.2 broadcast_select_fusion
  51.4 7.1 %all-to-all-start = ((bf16[16,32,1152]{2,1,0:T(8,128)(2,1)}), bf16[16,32,1152]{2,1,0:T(8,128)(2,1)S(1)}, u32[]{:S(2)}, u32[]{:S(2)}) async-start(bf16[16,32,1152]{2,1,0:T(8,128)(2,1)} %broadcast_select_fusion), calls=%async_computation | async-start | bytes 2359296 | tf_op jit(solution)/shard_map/all_to_all | solution.py:51
  58.9 2.5 %copy.36 = bf16[16,32,3,12,3,1]{3,2,4,5,1,0:T(4,128)(2,1)} copy(bf16[16,32,3,12,3,1]{1,0,4,3,2,5:T(8,128)(2,1)S(1)} %bitcast.61) | data formatting | bytes 221184 | tf_op jit(solution)/shard_map/reshape;squeeze | solution.py:26
  61.5 23.7 %all-to-all-done = bf16[16,32,1152]{2,1,0:T(8,128)(2,1)S(1)} async-done(((bf16[16,32,1152]{2,1,0:T(8,128)(2,1)}), bf16[16,32,1152]{2,1,0:T(8,128)(2,1)S(1)}, u32[]{:S(2)}, u32[]{:S(2)}) %all-to-all-start) | async-done | bytes 1179680 | tf_op jit(solution)/shard_map/all_to_all | solution.py:51
  85.3 3.3 %copy.25 = bf16[16,32,1152]{1,2,0:T(8,128)(2,1)} copy(bf16[16,32,1152]{2,1,0:T(8,128)(2,1)S(1)} %all-to-all-done) | data formatting | bytes 2359296 | tf_op jit(solution)/shard_map/all_to_all | solution.py:51
  88.6 19.6 %copy.27 = bf16[16,32,12,2,3,16]{5,2,4,3,1,0:T(8,128)(2,1)} copy(bf16[16,32,12,2,3,16]{1,5,4,3,2,0:T(8,128)(2,1)} %bitcast.58) | data formatting | bytes 2359296 | tf_op jit(solution)/shard_map/reshape | solution.py:27
  108.3 6.6 %convolution_bitcast_fusion = f32[3,16,32,2,16]{4,0,3,2,1:T(4,128)} fusion(bf16[16,32,12,2,3,16]{5,2,4,3,1,0:T(8,128)(2,1)} %copy.27, bf16[16,32,3,12,3,1]{3,2,4,5,1,0:T(4,128)(2,1)S(1)} %copy-done.1), kind=kOutput, calls=%fused_computation.10 | convolution fusion | flops 3538944 | bytes 1486848 | tf_op jit(solution)/shard_map/scepk,scpikh->escih/dot_general | solution.py:28
  114.9 1.8 %copy.29 = f32[3,16,32,2,16]{2,1,0,4,3:T(8,128)S(1)} copy(f32[3,16,32,2,16]{4,0,3,2,1:T(4,128)} %convolution_bitcast_fusion) | data formatting | bytes 393216 | tf_op jit(solution)/shard_map/scepk,scpikh->escih/transpose | solution.py:28
  117.1 2.2 %fusion.2 = f32[32,384]{0,1:T(8,128)S(1)} fusion(f32[1536,32]{0,1:T(8,128)S(1)} %reshape.104, s32[1536]{0:T(1024)S(1)} %eq.15), kind=kOutput, calls=%fused_computation.8 | convolution fusion | flops 227082240 | bytes 251904 | tf_op jit(solution)/shard_map/ra,re->ae/dot_general | solution.py:58
  119.3 0.6 gather_fusion.1
  119.9 5.4 %collective-permute-start = (f32[32,32]{0,1:T(8,128)S(1)}, f32[32,32]{0,1:T(8,128)S(1)}, u32[]{:S(2)}, u32[]{:S(2)}) collective-permute-start(f32[32,32]{0,1:T(8,128)S(1)} %bitcast.63), channel_id=1, source_target_pairs={{0,2},{2,4},{4,6},{6,8},{8,10},{10,12},{12,14},{14,16},{16,18},{18... | collective-permute-start | bytes 12296 | tf_op jit(solution)/shard_map/ppermute | solution.py:18
  125.9 1.9 %collective-permute-start.1 = (f32[32,32]{0,1:T(8,128)S(1)}, f32[32,32]{0,1:T(8,128)S(1)}, u32[]{:S(2)}, u32[]{:S(2)}) collective-permute-start(f32[32,32]{0,1:T(8,128)S(1)} %bitcast.62), channel_id=1, source_target_pairs={{2,0},{4,2},{6,4},{8,6},{10,8},{12,10},{14,12},{16,14},{18,16},{20... | collective-permute-start | bytes 12296 | tf_op jit(solution)/shard_map/ppermute | solution.py:19
  127.8 0.8 scatter_custom_fusion
  128.7 4.6 %collective-permute-done.1 = f32[32,32]{0,1:T(8,128)S(1)} collective-permute-done((f32[32,32]{0,1:T(8,128)S(1)}, f32[32,32]{0,1:T(8,128)S(1)}, u32[]{:S(2)}, u32[]{:S(2)}) %collective-permute-start.1) | collective-permute-done | bytes 4128 | tf_op jit(solution)/shard_map/ppermute | solution.py:19
  133.3 0.8 scatter_custom_fusion.1
  134.2 0.7 copy.33
  (24 shorter events, 1.6 us)
Async XLA Ops:
  6.5 1.1 copy-start
  6.5 22.5 %all-gather.3.cloned.1.call-start = ((), (), s32[]{:S(2)}) async-start(), calls=%async_computation.1 | async-start | bytes 7077888 | tf_op jit(solution)/shard_map/all_gather | solution.py:39
  13.0 0.7 copy-start.3
  50.1 8.4 %copy-start.2 = (bf16[1,16,32,108]{3,2,1,0:T(8,128)(2,1)S(1)}, bf16[1,16,32,108]{3,2,1,0:T(8,128)(2,1)}, u32[]{:S(2)}) copy-start(bf16[1,16,32,108]{3,2,1,0:T(8,128)(2,1)} %param.9) | copy-start | bytes 331780
  51.4 10.0 %copy-start.4 = (s32[3,1,16,32]{3,2,1,0:T(8,128)S(1)}, s32[3,1,16,32]{3,2,1,0:T(8,128)}, u32[]{:S(2)}) copy-start(s32[3,1,16,32]{3,2,1,0:T(8,128)} %param.10) | copy-start | bytes 18436
  51.4 10.1 %copy-start.5 = (s32[1,2,32]{2,1,0:T(2,128)S(1)}, s32[1,2,32]{2,1,0:T(2,128)}, u32[]{:S(2)}) copy-start(s32[1,2,32]{2,1,0:T(2,128)} %param.11) | copy-start | bytes 772
  51.4 33.9 %all-to-all-start = ((bf16[16,32,1152]{2,1,0:T(8,128)(2,1)}), bf16[16,32,1152]{2,1,0:T(8,128)(2,1)S(1)}, u32[]{:S(2)}, u32[]{:S(2)}) async-start(bf16[16,32,1152]{2,1,0:T(8,128)(2,1)} %broadcast_select_fusion), calls=%async_computation | async-start | bytes 2359296 | tf_op jit(solution)/shard_map/all_to_all | solution.py:51
  88.6 19.7 %copy-start.1 = (bf16[16,32,3,12,3,1]{3,2,4,5,1,0:T(4,128)(2,1)S(1)}, bf16[16,32,3,12,3,1]{3,2,4,5,1,0:T(4,128)(2,1)}, u32[]{:S(2)}) copy-start(bf16[16,32,3,12,3,1]{3,2,4,5,1,0:T(4,128)(2,1)} %copy.36) | copy-start | bytes 331780
  119.9 7.9 %collective-permute-start = (f32[32,32]{0,1:T(8,128)S(1)}, f32[32,32]{0,1:T(8,128)S(1)}, u32[]{:S(2)}, u32[]{:S(2)}) collective-permute-start(f32[32,32]{0,1:T(8,128)S(1)} %bitcast.63), channel_id=1, source_target_pairs={{0,2},{2,4},{4,6},{6,8},{8,10},{10,12},{12,14},{14,16},{16,18},{18... | collective-permute-start | bytes 12296 | tf_op jit(solution)/shard_map/ppermute | solution.py:18
  125.9 7.4 %collective-permute-start.1 = (f32[32,32]{0,1:T(8,128)S(1)}, f32[32,32]{0,1:T(8,128)S(1)}, u32[]{:S(2)}, u32[]{:S(2)}) collective-permute-start(f32[32,32]{0,1:T(8,128)S(1)} %bitcast.62), channel_id=1, source_target_pairs={{2,0},{4,2},{6,4},{8,6},{10,8},{12,10},{14,12},{16,14},{18,16},{20... | collective-permute-start | bytes 12296 | tf_op jit(solution)/shard_map/ppermute | solution.py:19
Sparse Core Ops, SparseCore 0:
  13.2 15.8 all-gather.2
